TPU v7x, 32 devices: a whole 2x2x4 slice. The times are simulated.
32 devices in a mesh: groups: 2 (over y), row: 4 (over x, core), col: 4 (over z).
Axes of the slice: x: 2, y: 2, z: 4, core: 2. Of those that a mesh axis runs over, the one named last changes fastest.
Arguments:
- basis_values: bfloat16 [4, 4, 2048, 1536], P('row', 'col'), may hold values from -6 to 6
- potential: float32 [4, 4, 2048], P('row', 'col'), may hold values from -0.125 to 0.125
- basis_blocks: int32 [4, 4, 12], P('row', 'col'), may hold values from 0 to 63, as said below
- factor: bfloat16 [16, 4, 128, 1024], P(None, 'row', None, 'col'), may hold values from -0.1875 to 0.1875
Outputs:
- hamiltonian: float32 [32, 4, 16, 4, 128, 128], P('groups', 'row', None, 'col'), parts along dimension 0
- product: float32 [32, 4, 128, 16, 4, 128], P('groups', 'row', None, None, 'col'), parts along dimension 0
There are 2 independent parts, one for each index of `groups`. A program takes and returns all parts, laid end to end along the dimension named above; an argument that names none is the same for every part. Nothing has to cross between parts.
Inputs may be any that keep to these rules, and one draw needn't show every extreme that they name: `basis_blocks`: the 12 blocks of one batch are distinct and lie within 16 consecutive blocks counted cyclically over the 64 blocks of the window; every such range starts at one common offset modulo 16, and every block of the range whose position in it is a multiple of 4 is on the list. Hence at most 16 of a batch's block pairs (I, J) share the same (I mod 4, J mod 4), and some pair of residues has exactly 16.
All inputs are finite; a program needn't handle non-finite values.
Results may differ from a plain program's by a relative error of at most 0.0048.
Values may be sent and summed in bfloat16 or wider, within the bound.
A program may use at most 128 MiB of HBM per device.

v0:
```python
import jax
import jax.numpy as jnp
from jax import lax
from jax.sharding import PartitionSpec as P

NB = 8192
WIN = 16


def from_root(value, axis, source):
    kept = jnp.where(lax.axis_index(axis) == source, value, 0).astype(value.dtype)
    return lax.psum(kept, axis)


def slot_ranks(targets, usable):
    count = targets.shape[0]
    order = jnp.arange(count)
    earlier = order[None, :] < order[:, None]
    same_target = (targets[:, None] == targets[None, :]) & usable[None, :] & earlier
    return jnp.sum(same_target.astype(jnp.int32), axis=1)


def pack_slots(slot_of_item, slot_count, items, labels):
    selector = jnp.arange(slot_count)[:, None] == slot_of_item[None, :]
    packed = jnp.dot(
        selector.astype(jnp.bfloat16), items, preferred_element_type=jnp.float32
    ).astype(jnp.bfloat16)
    slot_labels = jnp.sum(jnp.where(selector, labels[None, :] + 1, 0), axis=1) - 1
    return (packed, slot_labels)


def sum_into_tile(received, received_labels, tile_blocks):
    selector = received_labels[:, None] == jnp.arange(tile_blocks)[None, :]
    return lax.dot_general(
        selector.astype(jnp.bfloat16),
        received,
        (((0,), (0,)), ((), ())),
        preferred_element_type=jnp.float32,
    )


def local(basis_values, potential, basis_blocks, factor):
    row_count = lax.axis_size("row")
    col_count = lax.axis_size("col")
    device_count = row_count * col_count
    phi_batch = basis_values[0, 0]
    weight_batch = potential[0, 0]
    block_list = basis_blocks[0, 0]
    list_length = block_list.shape[0]
    block_size = factor.shape[2]
    block_area = block_size * block_size
    window = WIN
    total_blocks = NB // block_size
    local_rows = total_blocks // row_count
    local_cols = total_blocks // col_count
    tile_blocks = local_rows * local_cols
    weighted = (phi_batch * weight_batch[:, None]).astype(jnp.bfloat16)
    partial_sum = lax.dot_general(
        phi_batch, weighted, (((0,), (0,)), ((), ())), preferred_element_type=jnp.float32
    ).astype(jnp.bfloat16)
    pieces = partial_sum.reshape(list_length, block_size, list_length, block_size).transpose(
        0, 2, 1, 3
    )
    row_share = min(list_length, window // row_count)
    col_share = min(list_length, window // col_count)
    row_label = jnp.broadcast_to(block_list[:, None], (list_length, list_length)).reshape(-1)
    col_label = jnp.broadcast_to(block_list[None, :], (list_length, list_length)).reshape(-1)
    owner = row_label % row_count * col_count + col_label % col_count
    capacity = row_share * col_share
    usable = jnp.ones(owner.shape, bool)
    slot_of_item = owner * capacity + slot_ranks(owner, usable)
    local_label = row_label // row_count * local_cols + col_label // col_count
    packed, slot_labels = pack_slots(
        slot_of_item,
        device_count * capacity,
        pieces.reshape(list_length * list_length, block_area),
        local_label,
    )
    packed = packed.reshape(device_count, capacity, block_area)
    slot_labels = slot_labels.reshape(device_count, capacity)
    received, received_labels = (
        lax.all_to_all(packed, ("row", "col"), split_axis=0, concat_axis=0, tiled=True),
        lax.all_to_all(slot_labels, ("row", "col"), split_axis=0, concat_axis=0, tiled=True),
    )
    tile = sum_into_tile(received.reshape(-1, block_area), received_labels.reshape(-1), tile_blocks)
    tile = tile.reshape(local_rows, local_cols, block_size, block_size)
    hamiltonian = tile.reshape(local_rows, 1, local_cols, 1, block_size, block_size)
    tile_narrow = tile.astype(jnp.bfloat16)
    head_width = factor.shape[3] * col_count
    head_blocks = head_width // block_size
    gathered_rows = []
    for block_row in range(head_blocks):
        gathered_rows.append(
            from_root(tile_narrow[block_row // row_count], "row", block_row % row_count)
        )
    head_stack = jnp.stack(gathered_rows, axis=0)
    head_matrix = head_stack.transpose(0, 2, 1, 3).reshape(head_width, local_cols * block_size)
    piece = lax.all_gather(factor, "col", axis=3, tiled=True)
    width = piece.shape[3]
    product = jnp.dot(
        piece.reshape(local_rows * block_size, width),
        head_matrix,
        preferred_element_type=jnp.float32,
    )
    product = product.reshape(local_rows, 1, block_size, local_cols, 1, block_size)
    return (hamiltonian, product)


def solution(mesh):
    return jax.shard_map(
        local,
        mesh=mesh,
        in_specs=(
            P("row", "col", None, None),
            P("row", "col", None),
            P("row", "col", None),
            P(None, "row", None, "col"),
        ),
        out_specs=(
            P("groups", "row", None, "col", None, None),
            P("groups", "row", None, None, "col", None),
        ),
        check_vma=False,
    )
```

profile of v0, /device:TPU:0, one launch (start us, length us, event | category | flops | bytes accessed | tf_op | source)
XLA Modules:
  0.0 423.9 jit_solution(7756939959881441454)
XLA Ops:
  8.0 0.7 broadcast_in_dim.45
  8.7 0.1 reshape.286
  8.7 0.7 broadcast_in_dim.44
  9.5 0.1 reshape.285
  9.6 0.2 convert_reduce_fusion
  9.8 0.1 select_reduce_fusion
  9.9 0.7 sub.19
  10.6 7.4 %all-to-all-start = ((s32[16,1,16]{2,1,0:T(1,128)}), s32[16,1,16]{2,1,0:T(1,128)S(1)}, u32[]{:S(2)}, u32[]{:S(2)}) async-start(s32[16,1,16]{2,1,0:T(1,128)} %sub.19), calls=%async_computation | async-start | bytes 16384 | tf_op jit(solution)/shard_map/all_to_all | solution.py:83
  18.0 15.6 %fusion = bf16[1536,1536]{0,1:T(8,128)(2,1)} fusion(bf16[1,1,2048,1536]{3,2,1,0:T(8,128)(2,1)} %param.4, f32[2048]{0:T(1024)} %bitcast.89), kind=kOutput, calls=%fused_computation.4 | convolution fusion | flops 9675472896 | bytes 11018240 | tf_op jit(solution)/shard_map/dot_general | solution.py:58
  33.6 6.6 %copy.20 = bf16[1536,1536]{1,0:T(8,128)(2,1)} copy(bf16[1536,1536]{0,1:T(8,128)(2,1)} %fusion) | data formatting | bytes 9437184 | tf_op jit(solution)/shard_map/convert_element_type | solution.py:60
  40.2 9.4 %reshape.287 = bf16[12,128,12,128]{3,2,1,0:T(8,128)(2,1)} reshape(bf16[1536,1536]{1,0:T(8,128)(2,1)} %copy.20) | data formatting | bytes 9437184 | tf_op jit(solution)/shard_map/reshape | solution.py:61
  49.6 4.1 copy.21
  53.8 7.4 %convolution_convert_fusion = bf16[256,16384]{1,0:T(8,128)(2,1)} fusion(bf16[18,8,128,128]{3,2,1,0:T(8,128)(2,1)S(1)} %bitcast.76, s32[144]{0:T(256)S(1)} %multiply_add_fusion), kind=kOutput, calls=%fused_computation | convolution fusion | flops 1212190720 | bytes 13107776 | tf_op jit(solution)/shard_map/dot_general | solution.py:25
  61.2 0.0 all-to-all-done
  61.2 6.1 %all-to-all-start.1 = ((bf16[16,16,16384]{2,1,0:T(8,128)(2,1)}), bf16[16,16,16384]{2,1,0:T(8,128)(2,1)}, u32[]{:S(2)}, u32[]{:S(2)}) async-start(bf16[16,16,16384]{2,1,0:T(8,128)(2,1)} %bitcast.74), calls=%async_computation.1 | async-start | bytes 16777216 | tf_op jit(solution)/shard_map/all_to_all | solution.py:82
  67.3 0.2 all-reduce.3.cloned.1.call-start
  67.5 0.5 broadcast.328
  68.0 0.7 reduce.3
  68.7 0.1 eq.66
  68.8 182.8 %all-to-all-done.1 = bf16[16,16,16384]{2,1,0:T(8,128)(2,1)} async-done(((bf16[16,16,16384]{2,1,0:T(8,128)(2,1)}), bf16[16,16,16384]{2,1,0:T(8,128)(2,1)}, u32[]{:S(2)}, u32[]{:S(2)}) %all-to-all-start.1) | async-done | bytes 8388640 | tf_op jit(solution)/shard_map/all_to_all | solution.py:82
  251.6 12.0 %fusion.17 = (bf16[256,16384]{1,0:T(8,128)(2,1)S(1)}, f32[256,16384]{1,0:T(8,128)}) fusion(bf16[256,16384]{1,0:T(8,128)(2,1)} %bitcast.7, s32[256]{0:T(256)S(1)} %eq.66), kind=kOutput, calls=%fused_computation.57 | convolution fusion | flops 2151743488 | bytes 33555456 | tf_op jit(solution)/shard_map/dot_general | solution.py:34
  263.6 0.3 select_bitcast_fusion
  263.9 0.1 copy.41
  264.0 1.2 copy.29
  265.1 0.1 copy.35
  265.2 1.2 copy.23
  266.4 0.1 copy.36
  266.5 1.1 copy.24
  267.6 0.1 copy.39
  267.7 1.1 copy.27
  268.9 0.1 copy.40
  269.0 1.1 copy.28
  270.1 0.1 copy.38
  270.2 1.2 copy.26
  271.3 0.1 copy.34
  271.4 1.2 copy.22
  272.6 0.1 copy.37
  272.7 1.1 copy.25
  273.8 0.0 all-reduce.3.cloned.1.call-update
  273.9 0.3 all-gather.2.cloned.1.call-start
  274.1 0.3 all-gather.2.cloned.1.call-update
  274.4 14.3 %copy.33 = f32[32,8,128,128]{3,2,1,0:T(8,128)} copy(f32[32,8,128,128]{3,1,2,0:T(8,128)} %bitcast.72) | data formatting | bytes 33554432
  288.8 70.7 %all-reduce.3.cloned.1.call-done = (bf16[1,16,128,128]{3,1,2,0:T(8,128)(2,1)}, bf16[1,16,128,128]{3,1,2,0:T(8,128)(2,1)}, bf16[1,16,128,128]{3,1,2,0:T(8,128)(2,...) async-done(((bf16[1,16,128,128]{3,1,2,0:T(8,128)(2,1)}, ...) | async-done | bytes 4194320 | tf_op jit(solution)/shard_map/psum | solution.py:12
  359.5 0.0 copy-start.2
  359.5 0.0 copy-start.1
  359.5 0.0 copy-start
  359.5 2.0 constant_dynamic-update-slice_fusion.7
  361.5 1.9 constant_dynamic-update-slice_fusion.6
  363.3 1.9 constant_dynamic-update-slice_fusion.5
  365.2 1.9 constant_dynamic-update-slice_fusion.4
  367.1 1.9 constant_dynamic-update-slice_fusion.3
  368.9 0.0 copy-done.2
  368.9 0.8 constant_dynamic-update-slice_fusion.2
  369.8 0.0 copy-done.1
  369.8 0.8 constant_dynamic-update-slice_fusion.1
  370.6 0.0 copy-done
  370.6 0.8 constant_dynamic-update-slice_fusion
  371.4 0.0 all-gather.2.cloned.1.call-done
  371.4 12.6 %convolution_bitcast_fusion = f32[256,8,16,128]{3,1,2,0:T(8,128)S(1)} fusion(bf16[2048,1024]{1,0:T(8,128)(2,1)} %bitcast.88, bf16[128,8,16,128]{3,2,1,0:T(8,128)(2,1)} %bitcast.44), kind=kOutput, calls=%fused_computation.2 | convolution fusion | flops 8589934592 | bytes 25165824 | tf_op jit(solution)/shard_map/dot_general | solution.py:100
  384.0 7.5 %copy.43 = f32[256,8,16,128]{3,2,1,0:T(8,128)} copy(f32[256,8,16,128]{3,1,2,0:T(8,128)S(1)} %convolution_bitcast_fusion) | data formatting | bytes 33554432
  391.5 24.9 %copy.31 = f32[16,1,128,16,1,128]{5,4,3,2,1,0:T(1,128)} copy(f32[16,1,128,16,1,128]{2,0,5,3,4,1:T(8,128)} %bitcast.73) | data formatting | bytes 33554432
  (3 shorter events, 0.0 us)
Async XLA Ops:
  10.6 50.6 %all-to-all-start = ((s32[16,1,16]{2,1,0:T(1,128)}), s32[16,1,16]{2,1,0:T(1,128)S(1)}, u32[]{:S(2)}, u32[]{:S(2)}) async-start(s32[16,1,16]{2,1,0:T(1,128)} %sub.19), calls=%async_computation | async-start | bytes 16384 | tf_op jit(solution)/shard_map/all_to_all | solution.py:83
  61.2 190.4 %all-to-all-start.1 = ((bf16[16,16,16384]{2,1,0:T(8,128)(2,1)}), bf16[16,16,16384]{2,1,0:T(8,128)(2,1)}, u32[]{:S(2)}, u32[]{:S(2)}) async-start(bf16[16,16,16384]{2,1,0:T(8,128)(2,1)} %bitcast.74), calls=%async_computation.1 | async-start | bytes 16777216 | tf_op jit(solution)/shard_map/all_to_all | solution.py:82
  67.3 292.2 %all-reduce.3.cloned.1.call-start = ((), (), s32[]{:S(2)}) async-start(), calls=%async_computation.3 | async-start | bytes 8388608 | tf_op jit(solution)/shard_map/psum | solution.py:12
  273.9 97.6 %all-gather.2.cloned.1.call-start = ((), (), s32[]{:S(2)}) async-start(), calls=%async_computation.2 | async-start | bytes 5242880 | tf_op jit(solution)/shard_map/all_gather | solution.py:98
  359.5 9.5 %copy-start.2 = (bf16[1,16,128,128]{3,1,2,0:T(8,128)(2,1)S(1)}, bf16[1,16,128,128]{3,1,2,0:T(8,128)(2,1)}, u32[]{:S(2)}) copy-start(bf16[1,16,128,128]{3,1,2,0:T(8,128)(2,1)} %get-tuple-element.13) | copy-start | bytes 1572868
  359.5 10.3 %copy-start.1 = (bf16[1,16,128,128]{3,1,2,0:T(8,128)(2,1)S(1)}, bf16[1,16,128,128]{3,1,2,0:T(8,128)(2,1)}, u32[]{:S(2)}) copy-start(bf16[1,16,128,128]{3,1,2,0:T(8,128)(2,1)} %get-tuple-element.14) | copy-start | bytes 1572868
  359.5 11.1 %copy-start = (bf16[1,16,128,128]{3,1,2,0:T(8,128)(2,1)S(1)}, bf16[1,16,128,128]{3,1,2,0:T(8,128)(2,1)}, u32[]{:S(2)}) copy-start(bf16[1,16,128,128]{3,1,2,0:T(8,128)(2,1)} %get-tuple-element.15) | copy-start | bytes 1572868
Sparse Core Ops, SparseCore 0:
  274.0 85.4 all-reduce.2
Sparse Core Ops, SparseCore 1:
  275.9 79.1 all-gather.1
where the time goes:
time: 425 us; the launch traced here: 424 us
  waiting for transfers between devices  254 us (60%)
  local copies, waits for them, and re-layouts  91.6 us (22%)
  matrix products  47.6 us (11%)
  between operations  15.6 us (4%)
  starting transfers between devices  13.9 us (3%)
    all_to_all x1, waiting for transfers between devices, local(): lax.all_to_all(packed, ('row', 'col'), split_axis=0, concat_axis=0, tiled...  183 us
    psum x1, waiting for transfers between devices, from_root(): return lax.psum(kept, axis)  70.7 us
    unnamed x24, local copies, waits for them, and re-layouts  58.6 us
    dot_general x1, matrix products, local(): lax.dot_general(phi_batch, weighted, (((0,), (0,)), ((), ())), preferred_...  15.6 us
    dot_general x1, matrix products, local(): jnp.dot(piece.reshape(local_rows * block_size, width), head_matrix, prefe...  12.6 us
    dot_general x1, matrix products, sum_into_tile(): lax.dot_general(selector.astype(jnp.bfloat16), received, (((0,), (0,)), (...  12 us
    another operation x9, local copies, waits for them, and re-layouts, local(): head_stack = jnp.stack(gathered_rows, axis=0)  10 us
    reshape x1, local copies, waits for them, and re-layouts, local(): partial_sum.reshape(list_length, block_size, list_length, block_size)  9.42 us
  transfers between devices with their start and end apart: 4, of which 2 were waited for; matrix products, arithmetic and copies ran while one was open for 17% of the time, Pallas kernels for 0%

commit v1 on v0

--- a/solution.py
+++ b/solution.py
@@ -2,14 +2,19 @@
 import jax.numpy as jnp
 from jax import lax
 from jax.sharding import PartitionSpec as P
+from jax.lax import all_gather
 
 NB = 8192
 WIN = 16
 
 
+def apply_the_counts(local_block, peer_axis):
+    return all_gather(local_block, peer_axis).sum(axis=0)
+
+
 def from_root(value, axis, source):
     kept = jnp.where(lax.axis_index(axis) == source, value, 0).astype(value.dtype)
-    return lax.psum(kept, axis)
+    return apply_the_counts(kept, axis)
 
 
 def slot_ranks(targets, usable):

time: 425 us -> 590 us (1.39)
  waiting for transfers between devices: 254 us -> 408 us
  other arithmetic: 1.28 us -> 20.1 us
  local copies, waits for them, and re-layouts: 91.6 us -> 85.3 us
    all_gather x0 -> x8, waiting for transfers between devices: none -> 152 us  [apply_the_counts(): return all_gather(local_block, peer_axis).sum(axis=0)]
    all_gather x1, waiting for transfers between devices: 0.01 us -> 71.7 us  [local(): piece = lax.all_gather(factor, 'col', axis=3, tiled=True)]
    psum x1 -> x0, waiting for transfers between devices: 70.7 us -> none  [from_root(): return lax.psum(kept, axis)]
    reduce_sum x0 -> x8, other arithmetic: none -> 18 us  [apply_the_counts(): return all_gather(local_block, peer_axis).sum(axis=0)]
    another operation x9 -> x1, local copies, waits for them, and re-layouts: 10 us -> 0.07 us  [local(): head_stack = jnp.stack(gathered_rows, axis=0)]
    unnamed x24 -> x18, local copies, waits for them, and re-layouts: 58.6 us -> 57.4 us
  transfers between devices with their start and end apart: 4 -> 11, of which waited for: 2 -> 9; matrix products, arithmetic and copies ran while one was open for 17% -> 16% of each run, Pallas kernels for 0% -> 0%
where the time goes in v1:
time: 590 us; the launch traced here: 589 us
  waiting for transfers between devices  408 us (69%)
  local copies, waits for them, and re-layouts  85.3 us (14%)
  matrix products  47.6 us (8%)
  other arithmetic  20.1 us (3%)
  starting transfers between devices  14 us (2%)
  between operations  14 us (2%)
    all_to_all x1, waiting for transfers between devices, local(): lax.all_to_all(packed, ('row', 'col'), split_axis=0, concat_axis=0, tiled...  183 us
    all_gather x8, waiting for transfers between devices, apply_the_counts(): return all_gather(local_block, peer_axis).sum(axis=0)  152 us
    all_gather x1, waiting for transfers between devices, local(): piece = lax.all_gather(factor, 'col', axis=3, tiled=True)  71.7 us
    unnamed x18, local copies, waits for them, and re-layouts  57.4 us
    reduce_sum x8, other arithmetic, apply_the_counts(): return all_gather(local_block, peer_axis).sum(axis=0)  18 us
    dot_general x1, matrix products, local(): lax.dot_general(phi_batch, weighted, (((0,), (0,)), ((), ())), preferred_...  15.6 us
    dot_general x1, matrix products, local(): jnp.dot(piece.reshape(local_rows * block_size, width), head_matrix, prefe...  12.6 us
    dot_general x1, matrix products, sum_into_tile(): lax.dot_general(selector.astype(jnp.bfloat16), received, (((0,), (0,)), (...  12 us
  transfers between devices with their start and end apart: 11, of which 9 were waited for; matrix products, arithmetic and copies ran while one was open for 16% of the time, Pallas kernels for 0%

profile of v1, /device:TPU:0, one launch (start us, length us, event | category | flops | bytes accessed | tf_op | source)
XLA Modules:
  0.0 588.7 jit_solution(6911053354208654765)
XLA Ops:
  7.2 0.7 broadcast_in_dim.45
  7.8 0.1 reshape.254
  7.9 0.7 broadcast_in_dim.44
  8.6 0.1 reshape.253
  8.7 0.2 convert_reduce_fusion
  8.9 0.1 select_reduce_fusion
  9.1 0.7 sub.19
  9.8 7.4 %all-to-all-start = ((s32[16,1,16]{2,1,0:T(1,128)}), s32[16,1,16]{2,1,0:T(1,128)S(1)}, u32[]{:S(2)}, u32[]{:S(2)}) async-start(s32[16,1,16]{2,1,0:T(1,128)} %sub.19), calls=%async_computation | async-start | bytes 16384 | tf_op jit(solution)/shard_map/all_to_all | solution.py:88
  17.1 15.6 %fusion = bf16[1536,1536]{0,1:T(8,128)(2,1)} fusion(bf16[1,1,2048,1536]{3,2,1,0:T(8,128)(2,1)} %param.4, f32[2048]{0:T(1024)} %bitcast.107), kind=kOutput, calls=%fused_computation.4 | convolution fusion | flops 9675472896 | bytes 11018240 | tf_op jit(solution)/shard_map/dot_general | solution.py:63
  32.8 6.6 %copy.17 = bf16[1536,1536]{1,0:T(8,128)(2,1)} copy(bf16[1536,1536]{0,1:T(8,128)(2,1)} %fusion) | data formatting | bytes 9437184 | tf_op jit(solution)/shard_map/convert_element_type | solution.py:65
  39.4 9.4 %reshape.255 = bf16[12,128,12,128]{3,2,1,0:T(8,128)(2,1)} reshape(bf16[1536,1536]{1,0:T(8,128)(2,1)} %copy.17) | data formatting | bytes 9437184 | tf_op jit(solution)/shard_map/reshape | solution.py:66
  48.8 4.1 copy.18
  52.9 7.4 %convolution_convert_fusion = bf16[256,16384]{1,0:T(8,128)(2,1)} fusion(bf16[18,8,128,128]{3,2,1,0:T(8,128)(2,1)S(1)} %bitcast.92, s32[144]{0:T(256)S(1)} %multiply_add_fusion), kind=kOutput, calls=%fused_computation | convolution fusion | flops 1212190720 | bytes 13107776 | tf_op jit(solution)/shard_map/dot_general | solution.py:30
  60.4 6.1 %all-to-all-start.1 = ((bf16[16,16,16384]{2,1,0:T(8,128)(2,1)}), bf16[16,16,16384]{2,1,0:T(8,128)(2,1)}, u32[]{:S(2)}, u32[]{:S(2)}) async-start(bf16[16,16,16384]{2,1,0:T(8,128)(2,1)} %bitcast.90), calls=%async_computation.1 | async-start | bytes 16777216 | tf_op jit(solution)/shard_map/all_to_all | solution.py:87
  66.4 0.2 all-gather.24.cloned.1.call-start
  66.7 0.5 broadcast.312
  67.2 0.7 reduce.11
  67.8 0.1 eq.66
  67.9 182.8 %all-to-all-done.1 = bf16[16,16,16384]{2,1,0:T(8,128)(2,1)} async-done(((bf16[16,16,16384]{2,1,0:T(8,128)(2,1)}), bf16[16,16,16384]{2,1,0:T(8,128)(2,1)}, u32[]{:S(2)}, u32[]{:S(2)}) %all-to-all-start.1) | async-done | bytes 8388640 | tf_op jit(solution)/shard_map/all_to_all | solution.py:87
  250.7 12.0 %fusion.17 = (bf16[256,16384]{1,0:T(8,128)(2,1)S(1)}, f32[256,16384]{1,0:T(8,128)}) fusion(bf16[256,16384]{1,0:T(8,128)(2,1)} %bitcast.7, s32[256]{0:T(256)S(1)} %eq.66), kind=kOutput, calls=%fused_computation.57 | convolution fusion | flops 2151743488 | bytes 33555456 | tf_op jit(solution)/shard_map/dot_general | solution.py:39
  262.7 1.1 select_bitcast_fusion
  263.8 0.9 copy.31
  264.7 0.0 all-gather.12.cloned.1.call-start
  264.8 1.9 copy.25
  266.8 0.0 all-gather.14.cloned.1.call-start
  266.8 0.9 copy.26
  267.8 0.0 all-gather.20.cloned.1.call-start
  267.8 0.9 copy.29
  268.7 0.0 all-gather.22.cloned.1.call-start
  268.8 0.9 copy.30
  269.7 0.9 copy.28
  270.7 0.9 copy.24
  271.6 0.0 all-gather.16.cloned.1.call-start
  271.7 0.9 copy.27
  272.7 0.7 all-gather.26.cloned.1.call-update
  273.4 14.2 %copy.23 = f32[32,8,128,128]{3,2,1,0:T(8,128)} copy(f32[32,8,128,128]{3,1,2,0:T(8,128)} %bitcast.88) | data formatting | bytes 33554432
  287.5 2.0 reduce_sum.123
  289.6 20.8 %all-gather.12.cloned.1.call-done = bf16[4,16,128,128]{3,2,1,0:T(8,128)(2,1)} async-done(((bf16[1,16,128,128]{3,2,1,0:T(8,128)(2,1)}), bf16[4,16,128,128]{3,2,1,0:T(8,128)(2,1)}) %all-gather.12.cloned.1.call-update) | async-done | bytes 2097168 | tf_op jit(solution)/shard_map/all_gather | solution.py:12
  310.3 2.0 reduce_sum.117
  312.4 22.2 %all-gather.14.cloned.1.call-done = bf16[4,16,128,128]{3,2,1,0:T(8,128)(2,1)} async-done(((bf16[1,16,128,128]{3,2,1,0:T(8,128)(2,1)}), bf16[4,16,128,128]{3,2,1,0:T(8,128)(2,1)}) %all-gather.14.cloned.1.call-update) | async-done | bytes 2097168 | tf_op jit(solution)/shard_map/all_gather | solution.py:12
  334.5 2.0 reduce_sum.118
  336.5 22.0 %all-gather.20.cloned.1.call-done = bf16[4,16,128,128]{3,2,1,0:T(8,128)(2,1)} async-done(((bf16[1,16,128,128]{3,2,1,0:T(8,128)(2,1)}), bf16[4,16,128,128]{3,2,1,0:T(8,128)(2,1)}) %all-gather.20.cloned.1.call-update) | async-done | bytes 2097168 | tf_op jit(solution)/shard_map/all_gather | solution.py:12
  358.6 2.0 reduce_sum.121
  360.6 22.0 %all-gather.22.cloned.1.call-done = bf16[4,16,128,128]{3,2,1,0:T(8,128)(2,1)} async-done(((bf16[1,16,128,128]{3,2,1,0:T(8,128)(2,1)}), bf16[4,16,128,128]{3,2,1,0:T(8,128)(2,1)}) %all-gather.22.cloned.1.call-update) | async-done | bytes 2097168 | tf_op jit(solution)/shard_map/all_gather | solution.py:12
  382.6 2.0 reduce_sum.122
  384.6 22.0 %all-gather.18.cloned.1.call-done = bf16[4,16,128,128]{3,2,1,0:T(8,128)(2,1)} async-done(((bf16[1,16,128,128]{3,2,1,0:T(8,128)(2,1)}), bf16[4,16,128,128]{3,2,1,0:T(8,128)(2,1)}) %all-gather.18.cloned.1.call-update) | async-done | bytes 2097168 | tf_op jit(solution)/shard_map/all_gather | solution.py:12
  406.6 2.0 reduce_sum.120
  408.6 22.2 %all-gather.10.cloned.1.call-done = bf16[4,16,128,128]{3,2,1,0:T(8,128)(2,1)} async-done(((bf16[1,16,128,128]{3,2,1,0:T(8,128)(2,1)}), bf16[4,16,128,128]{3,2,1,0:T(8,128)(2,1)}) %all-gather.10.cloned.1.call-update) | async-done | bytes 2097168 | tf_op jit(solution)/shard_map/all_gather | solution.py:12
  430.8 2.9 reduce_sum.116
  433.7 21.3 %all-gather.16.cloned.1.call-done = bf16[4,16,128,128]{3,2,1,0:T(8,128)(2,1)} async-done(((bf16[1,16,128,128]{3,2,1,0:T(8,128)(2,1)}), bf16[4,16,128,128]{3,2,1,0:T(8,128)(2,1)}) %all-gather.16.cloned.1.call-update) | async-done | bytes 2097168 | tf_op jit(solution)/shard_map/all_gather | solution.py:12
  455.0 2.9 reduce_sum.119
  457.9 1.1 bitcast_dynamic-update-slice_fusion.7
  459.0 0.1 bitcast_dynamic-update-slice_fusion.6
  459.1 0.1 bitcast_dynamic-update-slice_fusion.5
  459.1 1.1 bitcast_dynamic-update-slice_fusion.4
  460.3 0.1 bitcast_dynamic-update-slice_fusion.3
  460.4 0.1 bitcast_dynamic-update-slice_fusion.2
  460.4 0.1 bitcast_dynamic-update-slice_fusion.1
  460.5 0.1 bitcast_dynamic-update-slice_fusion
  460.6 4.9 copy.19
  465.4 71.7 %all-gather.26.cloned.1.call-done = bf16[16,1,128,1024]{3,2,1,0:T(8,128)(2,1)} async-done(((bf16[16,1,128,256]{3,2,1,0:T(8,128)(2,1)}), bf16[16,1,128,1024]{3,2,1,0:T(8,128)(2,1)}) %all-gather.26.cloned.1.call-update) | async-done | bytes 4194320 | tf_op jit(solution)/shard_map/all_gather | solution.py:103
  537.2 12.6 %convolution_bitcast_fusion = f32[256,8,16,128]{3,1,2,0:T(8,128)S(1)} fusion(bf16[2048,1024]{1,0:T(8,128)(2,1)} %bitcast.106, bf16[128,8,16,128]{3,2,1,0:T(8,128)(2,1)} %bitcast.95), kind=kOutput, calls=%fused_computation.2 | convolution fusion | flops 8589934592 | bytes 25165824 | tf_op jit(solution)/shard_map/dot_general | solution.py:105
  549.8 7.5 %copy.33 = f32[256,8,16,128]{3,2,1,0:T(8,128)} copy(f32[256,8,16,128]{3,1,2,0:T(8,128)S(1)} %convolution_bitcast_fusion) | data formatting | bytes 33554432
  557.3 24.9 %copy.21 = f32[16,1,128,16,1,128]{5,4,3,2,1,0:T(1,128)} copy(f32[16,1,128,16,1,128]{2,0,5,3,4,1:T(8,128)} %bitcast.89) | data formatting | bytes 33554432
  (16 shorter events, 0.3 us)
Async XLA Ops:
  9.8 50.6 %all-to-all-start = ((s32[16,1,16]{2,1,0:T(1,128)}), s32[16,1,16]{2,1,0:T(1,128)S(1)}, u32[]{:S(2)}, u32[]{:S(2)}) async-start(s32[16,1,16]{2,1,0:T(1,128)} %sub.19), calls=%async_computation | async-start | bytes 16384 | tf_op jit(solution)/shard_map/all_to_all | solution.py:88
  60.4 190.4 %all-to-all-start.1 = ((bf16[16,16,16384]{2,1,0:T(8,128)(2,1)}), bf16[16,16,16384]{2,1,0:T(8,128)(2,1)}, u32[]{:S(2)}, u32[]{:S(2)}) async-start(bf16[16,16,16384]{2,1,0:T(8,128)(2,1)} %bitcast.90), calls=%async_computation.1 | async-start | bytes 16777216 | tf_op jit(solution)/shard_map/all_to_all | solution.py:87
  66.4 221.1 %all-gather.24.cloned.1.call-start = ((), (), s32[]{:S(2)}) async-start(), calls=%async_computation.9 | async-start | bytes 2621440 | tf_op jit(solution)/shard_map/all_gather | solution.py:12
  264.7 45.6 %all-gather.12.cloned.1.call-start = ((), (), s32[]{:S(2)}) async-start(), calls=%async_computation.3 | async-start | bytes 2621440 | tf_op jit(solution)/shard_map/all_gather | solution.py:12
  266.8 67.7 %all-gather.14.cloned.1.call-start = ((), (), s32[]{:S(2)}) async-start(), calls=%async_computation.4 | async-start | bytes 2621440 | tf_op jit(solution)/shard_map/all_gather | solution.py:12
  267.8 90.8 %all-gather.20.cloned.1.call-start = ((), (), s32[]{:S(2)}) async-start(), calls=%async_computation.7 | async-start | bytes 2621440 | tf_op jit(solution)/shard_map/all_gather | solution.py:12
  268.7 113.8 %all-gather.22.cloned.1.call-start = ((), (), s32[]{:S(2)}) async-start(), calls=%async_computation.8 | async-start | bytes 2621440 | tf_op jit(solution)/shard_map/all_gather | solution.py:12
  269.7 136.9 %all-gather.18.cloned.1.call-start = ((), (), s32[]{:S(2)}) async-start(), calls=%async_computation.6 | async-start | bytes 2621440 | tf_op jit(solution)/shard_map/all_gather | solution.py:12
  270.7 160.1 %all-gather.10.cloned.1.call-start = ((), (), s32[]{:S(2)}) async-start(), calls=%async_computation.2 | async-start | bytes 2621440 | tf_op jit(solution)/shard_map/all_gather | solution.py:12
  271.6 183.4 %all-gather.16.cloned.1.call-start = ((), (), s32[]{:S(2)}) async-start(), calls=%async_computation.5 | async-start | bytes 2621440 | tf_op jit(solution)/shard_map/all_gather | solution.py:12
  272.6 264.5 %all-gather.26.cloned.1.call-start = ((), (), s32[]{:S(2)}) async-start(), calls=%async_computation.10 | async-start | bytes 5242880 | tf_op jit(solution)/shard_map/all_gather | solution.py:103
Sparse Core Ops, SparseCore 0:
  264.9 21.2 all-gather.23
  287.7 22.5 all-gather.11
  311.9 22.5 all-gather.13
  335.9 22.5 all-gather.19
  360.0 22.5 all-gather.21
  384.0 22.5 all-gather.17
  408.2 22.5 all-gather.9
  432.4 22.5 all-gather.15
  456.6 80.5 all-gather.25
